TPU v7x, 512 devices: a whole 4x4x16 slice. The times are simulated.
512 devices in a mesh: grp: 16 (over x, y), dev: 32 (over z, core).
Axes of the slice: x: 4, y: 4, z: 16, core: 2. Of those that a mesh axis runs over, the one named last changes fastest.
Arguments:
- records: bfloat16 [131072, 128], P('grp', 'dev')
- dropout: int32 [131072, 128], P('grp', 'dev'), may hold values 0 or 1
- counts: int32 [512], P(('grp', 'dev')), may hold values from 128 to 256, as said below
Outputs:
- upper: float32 [512, 512], replicated
- basis: bfloat16 [131072, 512], P(('grp', 'dev'))
Inputs may be any that keep to these rules, and one draw needn't show every extreme that they name: `counts`: at least one time shard has all 256 rows valid.
All inputs are finite; a program needn't handle non-finite values. No bound on the sum of `dropout` on one device may be relied on, other than what follows from the above.
Results may differ from a plain program's by a relative error of at most 0.0012.
Values may be sent and summed in bfloat16 or wider, within the bound.
No kernel may reach another device: no remote copies, remote signals or barrier semaphores. Data moves between devices by JAX's collectives and lax.ppermute only.
A program may use at most 128 MiB of HBM per device.

v0:
```python
import jax
import jax.numpy as jnp
from jax import lax
from jax.sharding import PartitionSpec as P

LAGS = 4


def from_behind(value, axis, by):
    size = lax.axis_size(axis)
    pairs = [(i, i + by) for i in range(size) if 0 <= i + by < size]
    return lax.ppermute(value, axis, pairs)


def gram_term(piece):
    return lax.dot_general(
        piece, piece, (((0,), (0,)), ((), ())), preferred_element_type=jnp.float32
    )


def project(piece, high, low):
    first = jnp.dot(piece, high, preferred_element_type=jnp.float32)
    second = jnp.dot(piece, low, preferred_element_type=jnp.float32)
    return (first + second).astype(jnp.bfloat16)


def exact_dot(left, right):
    return jnp.dot(left, right, precision=lax.Precision.HIGHEST)


def factor_block(block):
    size = block.shape[0]
    augmented = jnp.concatenate([block, jnp.eye(size, dtype=jnp.float32)], axis=1)
    order = jnp.arange(size, dtype=jnp.int32)

    def eliminate(step, state):
        working, written = state
        pivot_row = lax.dynamic_slice_in_dim(working, step, 1, 0)[0]
        pivot = lax.dynamic_slice_in_dim(pivot_row, step, 1, 0)[0]
        scaled = pivot_row / jnp.sqrt(pivot)
        column = lax.dynamic_slice_in_dim(working, step, 1, 1)[:, 0]
        factor = jnp.where(order > step, column / pivot, jnp.zeros_like(column))
        working = working - factor[:, None] * pivot_row[None, :]
        written = lax.dynamic_update_slice_in_dim(written, scaled[None, :], step, 0)
        return (working, written)

    _, written = lax.fori_loop(0, size, eliminate, (augmented, jnp.zeros_like(augmented)))
    upper_block = jnp.triu(written[:, :size])
    lower_inverse = jnp.tril(written[:, size:])
    return (upper_block, lower_inverse)


def factor_parts(matrix):
    size = matrix.shape[0]
    panel = min(128, size)
    panels = size // panel
    working = matrix
    diag_blocks = []
    diag_inverses = []
    right_blocks = []
    for number in range(panels):
        upper_block, lower_inverse = factor_block(working[:panel, :panel])
        beside = exact_dot(lower_inverse, working[:panel, panel:])
        working = working[panel:, panel:] - exact_dot(jnp.transpose(beside), beside)
        diag_blocks.append(upper_block)
        diag_inverses.append(jnp.transpose(lower_inverse))
        right_blocks.append(beside)
    block_rows = []
    for number in range(panels):
        pieces = []
        if number > 0:
            pieces.append(jnp.zeros((panel, number * panel), jnp.float32))
        pieces.append(diag_blocks[number])
        if number + 1 < panels:
            pieces.append(right_blocks[number])
        block_rows.append(jnp.concatenate(pieces, axis=1))
    upper = jnp.concatenate(block_rows, axis=0)
    solved = [[None] * panels for number in range(panels)]
    for column in range(panels):
        solved[column][column] = diag_inverses[column]
        for row in range(column - 1, -1, -1):
            accum = jnp.zeros((panel, panel), jnp.float32)
            for middle in range(row + 1, column + 1):
                coupling = upper[
                    row * panel : (row + 1) * panel, middle * panel : (middle + 1) * panel
                ]
                accum = accum + exact_dot(coupling, solved[middle][column])
            solved[row][column] = -exact_dot(diag_inverses[row], accum)
    inverse_rows = []
    for row in range(panels):
        pieces = []
        for column in range(panels):
            if column < row:
                pieces.append(jnp.zeros((panel, panel), jnp.float32))
            else:
                pieces.append(solved[row][column])
        inverse_rows.append(jnp.concatenate(pieces, axis=1))
    return (upper, jnp.concatenate(inverse_rows, axis=0))


def shards(records, dropout, counts):
    local = (records.astype(jnp.float32) * dropout.astype(jnp.float32)).astype(jnp.bfloat16)
    series = lax.all_to_all(local, "dev", split_axis=0, concat_axis=1, tiled=True)
    rows = series.shape[0]
    ahead = from_behind(series[: LAGS - 1], ("grp", "dev"), -1)
    padded = jnp.concatenate([series, ahead], axis=0)
    hankel = jnp.concatenate([padded[k : k + rows] for k in range(LAGS)], axis=1)
    valid = jnp.arange(rows, dtype=jnp.int32) >= rows - counts[0]
    hankel = jnp.where(valid[:, None], hankel, jnp.zeros_like(hankel))
    total_rows = rows * lax.axis_size("grp") * lax.axis_size("dev")
    partial_value = gram_term(hankel)
    gram = lax.psum(partial_value, ("grp", "dev"))
    upper, inverse = factor_parts(gram / total_rows)
    high = inverse.astype(jnp.bfloat16)
    low = (inverse - lax.optimization_barrier(high).astype(jnp.float32)).astype(jnp.bfloat16)
    basis = project(hankel, high, low)
    return (upper, basis)


def solution(mesh):
    in_specs = (P("grp", "dev"), P("grp", "dev"), P(("grp", "dev")))
    out_specs = (P(), P(("grp", "dev"), None))
    return jax.shard_map(shards, mesh=mesh, in_specs=in_specs, out_specs=out_specs, check_vma=False)
```

profile of v0, /device:TPU:1, one launch (start us, length us, event | category | flops | bytes accessed | tf_op | source)
XLA Modules:
  0.0 1999.9 jit_solution(4296532873974421739)
XLA Ops:
  7.2 1.6 multiply_convert_fusion
  8.7 16.8 all-to-all-start
  26.2 12.4 all-to-all-done
  38.6 3.5 collective-permute-start
  42.1 1.7 collective-permute-done
  44.0 1.3 fusion.66
  45.4 462.2 %all-reduce.3.cloned.1.call-done = f32[512,512]{1,0:T(8,128)} async-done(((f32[512,512]{1,0:T(8,128)}), f32[512,512]{1,0:T(8,128)}) %all-reduce.3.cloned.1.call-update) | async-done | bytes 1048592 | tf_op jit(solution)/shard_map/psum | solution.py:112
  507.6 1.3 broadcast_multiply_fusion
  509.1 368.6 %while.76 = (s32[]{:T(128)}, f32[128,256]{0,1:T(8,128)S(1)}, f32[128,256]{0,1:T(8,128)S(1)}, s32[]{:T(128)}, s32[]{:T(128)}, /*index=5*/s32[]{:T(128)}, s32[]{:T(128)}) while((s32[]{:T(128)}, f32[128,256]{0,1:T(8,128)S(1)}, f32[128,256]{0,1:T(8,128)S(1)}, s32[]{:T(128)}, s32[]{:T(128)}, /*index=5*/s32[]{:T(128)}, s32[]{:T(128)}) %tuple.188), condition=%wide.region_2.3_spmd.clone, body=%wide.region_1.2_spmd.clone.sunk | while | flops 66180 | bytes 271501 | solution.py:47
  513.9 0.7 fusion.92
  522.6 0.7 fusion.92
  531.2 0.7 fusion.92
  539.8 0.7 fusion.92
  542.7 0.7 fusion.92
  548.5 0.7 fusion.92
  551.4 0.7 fusion.92
  560.0 0.7 fusion.92
  568.7 0.7 fusion.92
  577.3 0.7 fusion.92
  585.9 0.7 fusion.92
  594.6 0.7 fusion.92
  597.5 0.7 fusion.92
  603.2 0.7 fusion.92
  606.1 0.7 fusion.92
  614.7 0.7 fusion.92
  623.4 0.7 fusion.92
  632.0 0.7 fusion.92
  640.7 0.7 fusion.92
  649.3 0.7 fusion.92
  652.2 0.7 fusion.92
  657.9 0.7 fusion.92
  660.8 0.7 fusion.92
  669.5 0.7 fusion.92
  678.1 0.7 fusion.92
  686.8 0.7 fusion.92
  695.4 0.7 fusion.92
  704.0 0.7 fusion.92
  706.9 0.7 fusion.92
  712.7 0.7 fusion.92
  715.6 0.7 fusion.92
  724.2 0.7 fusion.92
  732.8 0.7 fusion.92
  878.0 0.7 convolution_subtract_fusion
  878.9 368.6 %while.77 = (s32[]{:T(128)}, f32[128,256]{0,1:T(8,128)S(1)}, f32[128,256]{0,1:T(8,128)S(1)}, s32[]{:T(128)}, s32[]{:T(128)}, /*index=5*/s32[]{:T(128)}, s32[]{:T(128)}) while((s32[]{:T(128)}, f32[128,256]{0,1:T(8,128)S(1)}, f32[128,256]{0,1:T(8,128)S(1)}, s32[]{:T(128)}, s32[]{:T(128)}, /*index=5*/s32[]{:T(128)}, s32[]{:T(128)}) %tuple.191), condition=%wide.region_4.5_spmd.clone, body=%wide.region_3.4_spmd.clone.sunk | while | flops 66180 | bytes 271501 | solution.py:47
  1248.6 368.6 %while.78 = (s32[]{:T(128)}, f32[128,256]{0,1:T(8,128)S(1)}, f32[128,256]{0,1:T(8,128)S(1)}, s32[]{:T(128)}, s32[]{:T(128)}, /*index=5*/s32[]{:T(128)}, s32[]{:T(128)}) while((s32[]{:T(128)}, f32[128,256]{0,1:T(8,128)S(1)}, f32[128,256]{0,1:T(8,128)S(1)}, s32[]{:T(128)}, s32[]{:T(128)}, /*index=5*/s32[]{:T(128)}, s32[]{:T(128)}) %tuple.194), condition=%wide.region_6.7_spmd.clone, body=%wide.region_5.6_spmd.clone.sunk | while | flops 66180 | bytes 271501 | solution.py:47
  1618.2 368.6 %while.79 = (s32[]{:T(128)}, f32[128,256]{0,1:T(8,128)S(1)}, f32[128,256]{0,1:T(8,128)S(1)}, s32[]{:T(128)}, s32[]{:T(128)}, /*index=5*/s32[]{:T(128)}, s32[]{:T(128)}) while((s32[]{:T(128)}, f32[128,256]{0,1:T(8,128)S(1)}, f32[128,256]{0,1:T(8,128)S(1)}, s32[]{:T(128)}, s32[]{:T(128)}, /*index=5*/s32[]{:T(128)}, s32[]{:T(128)}) %tuple.197), condition=%wide.region_8.9_spmd.clone, body=%wide.region_7.8_spmd.clone.sunk | while | flops 66180 | bytes 271501 | solution.py:47
  1990.8 1.1 fusion.12
  1992.0 1.1 fusion.16
  (2585 shorter events, 1082.8 us)
Async XLA Ops:
  8.7 29.8 %all-to-all-start = ((bf16[32,256,4]{1,2,0:T(4,128)(2,1)}), bf16[32,256,4]{1,2,0:T(4,128)(2,1)S(1)}, u32[]{:S(2)}, u32[]{:S(2)}) async-start(bf16[32,256,4]{1,2,0:T(4,128)(2,1)} %bitcast.1), calls=%async_computation | async-start | bytes 131072 | tf_op jit(solution)/shard_map/all_to_all | solution.py:103
  25.5 482.1 %all-reduce.3.cloned.1.call-start = ((), (), s32[]{:S(2)}) async-start(), calls=%async_computation.1 | async-start | bytes 2097152 | tf_op jit(solution)/shard_map/psum | solution.py:112
  38.6 5.2 collective-permute-start
Sparse Core Ops, SparseCore 0:
  45.4 462.1 all-reduce.2
where the time goes:
time: 2020 us; the launch traced here: 2000 us
  local copies, waits for them, and re-layouts  614 us (30%)
  other arithmetic  489 us (24%)
  waiting for transfers between devices  476 us (24%)
  loops' own time  377 us (19%)
  starting transfers between devices  20.3 us (1%)
    psum x1, waiting for transfers between devices, shards(): gram = lax.psum(partial_value, ('grp', 'dev'))  462 us
    another operation x4, loops' own time, factor_block(): lax.fori_loop(0, size, eliminate, (augmented, jnp.zeros_like(augmented)))  377 us
    mul x512, other arithmetic, eliminate(): working = working - factor[:, None] * pivot_row[None, :]  337 us
    dynamic_update_slice x512, local copies, waits for them, and re-layouts, eliminate(): written = lax.dynamic_update_slice_in_dim(written, scaled[None, :], step, 0)  312 us
    dynamic_slice x512, local copies, waits for them, and re-layouts, eliminate(): pivot = lax.dynamic_slice_in_dim(pivot_row, step, 1, 0)[0]  301 us
    div x512, other arithmetic, eliminate(): scaled = pivot_row / jnp.sqrt(pivot)  94.6 us
    sub x512, other arithmetic, eliminate(): working = working - factor[:, None] * pivot_row[None, :]  53.9 us
  transfers between devices with their start and end apart: 3, of which 3 were waited for; matrix products, arithmetic and copies ran while one was open for 0% of the time, Pallas kernels for 0%

commit v1 on v0

v1 whole, which is shorter than its diff:
```python
import jax
import jax.numpy as jnp
from jax import lax
from jax.experimental import pallas as pl
from jax.experimental.pallas import tpu as pltpu
from jax.sharding import PartitionSpec as P

f32, bf16 = jnp.float32, jnp.bfloat16

LAGS = 4
CHANNELS = 128
ROWS = 256
COLS = 512
TOTAL = 131072
GROUPS = 16
WINDOW = 640
PAIRS = [(i, j) for i in range(LAGS) for j in range(i, LAGS)]
HALF = 64
PACKED = HALF * len(PAIRS)
SLICE = PACKED // GROUPS

PARAMS = pltpu.CompilerParams(vmem_limit_bytes=48 * 2**20)
SMEM = pl.BlockSpec(memory_space=pltpu.SMEM)
VMEM = pl.BlockSpec(memory_space=pltpu.VMEM)


def split(x):
    high = x.astype(bf16)
    return high, (x - high.astype(f32)).astype(bf16)


def dot_tn(left, right):
    return lax.dot_general(left, right, (((0,), (0,)), ((), ())), preferred_element_type=f32)


def dot_nt(left, right):
    return lax.dot_general(left, right, (((1,), (1,)), ((), ())), preferred_element_type=f32)


def dot_nn(left, right):
    return jnp.dot(left, right, preferred_element_type=f32)


def triple(x, order, axis):
    high, low = split(x)
    return jnp.concatenate([low if c == "l" else high for c in order], axis=axis)


def pack_kernel(count, records, dropout, head, out):
    signal = (records[...].astype(f32) * dropout[...].astype(f32)).astype(bf16)
    lane = lax.broadcasted_iota(jnp.int32, (4, 128), 1)
    counted = jnp.full((4, 128), count[0], jnp.int32).astype(f32)
    for z in range(16):
        behind = signal[:, 512 * z + 512 : 512 * z + 640] if z < 15 else head[...]
        behind = jnp.where(lane == 127, counted, behind.astype(f32)).astype(bf16)
        for core in range(2):
            out[2 * z + core, :, 0:512] = signal[:, 512 * z : 512 * z + 512]
            out[2 * z + core, :, 512:640] = behind


def gram_kernel(place, series, packed, hankel, lagged):
    z, core = place[0], place[1]
    samples = series[...].astype(f32)
    source = lax.broadcasted_iota(jnp.int32, (CHANNELS, 1), 0)
    tail = samples[:, WINDOW - 1 : WINDOW]
    time = lax.broadcasted_iota(jnp.int32, (1, 512), 1)
    counts = [
        jnp.sum(jnp.where(source == 8 * z + 4 * e, tail, 0.0), axis=0, keepdims=True) for e in range(2)
    ]
    least = jnp.where(time < ROWS, ROWS - counts[0], 2 * ROWS - counts[1])
    valid = time.astype(f32) >= least
    for i in range(LAGS):
        moved = samples if i == 0 else pltpu.roll(samples, WINDOW - i, 1)
        lagged[CHANNELS * i : CHANNELS * (i + 1), :] = jnp.where(valid, moved[:, :512], 0.0).astype(bf16)
    every = lagged[...]
    mine = jnp.concatenate(
        [lagged[pl.ds(pl.multiple_of(CHANNELS * i + HALF * core, HALF), HALF), :] for i in range(LAGS)], axis=0
    )
    gram = dot_nt(mine, every)
    for b, (i, j) in enumerate(PAIRS):
        packed[HALF * b : HALF * (b + 1), :] = gram[HALF * i : HALF * (i + 1), CHANNELS * j : CHANNELS * (j + 1)]
    own = lagged[:, pl.ds(pl.multiple_of(ROWS * core, ROWS), ROWS)]
    hankel[...] = jnp.transpose(own.astype(f32)).astype(bf16)


def sum_kernel(parts, out):
    total = parts[0]
    for s in range(1, GROUPS):
        total = total + parts[s]
    for s in range(GROUPS):
        out[s] = total


def pivots(work, start):
    lanes = (8, 128)
    sub = lax.broadcasted_iota(jnp.int32, lanes, 0)
    parts = [work[start : start + 8, 0:128], work[start : start + 8, 128:256]]
    cols = [jnp.broadcast_to(parts[0][:, start + i : start + i + 1], lanes) for i in range(8)]
    scale = jnp.ones(lanes, f32)
    for k in range(8):
        pivot = jnp.broadcast_to(cols[k][k : k + 1, :], lanes)
        factor = jnp.where(sub > k, cols[k] * (1.0 / pivot), 0.0)
        scale = jnp.where(sub == k, lax.rsqrt(pivot), scale)
        for i in range(k + 1, 8):
            cols[i] = cols[i] - factor * jnp.broadcast_to(cols[i][k : k + 1, :], lanes)
        parts = [v - factor * jnp.broadcast_to(v[k : k + 1, :], lanes) for v in parts]
    return [v * scale for v in parts]


def factor_diag(work, rows):
    for start in range(0, 128, 8):
        done = jnp.concatenate(pivots(work, start), axis=1)
        rows[start : start + 8, :] = done
        if start < 120:
            high = done.astype(bf16).astype(f32)
            low = done - high
            left = jnp.concatenate([high[:, :128], high[:, :128], low[:, :128]], axis=0).astype(bf16)
            right = jnp.concatenate([high, low, high], axis=0).astype(bf16)
            change = dot_tn(left, right)
            work[start + 8 : 128, :] = work[start + 8 : 128, :] - change[start + 8 : 128, :]


def factor_kernel(place, own, other, hankel, upper, basis, gram, work, rows, behind):
    core = place[1]
    for b, (i, j) in enumerate(PAIRS):
        block = pl.ds(HALF * b, HALF)
        cols = pl.ds(CHANNELS * j, CHANNELS)
        gram[pl.ds(pl.multiple_of(CHANNELS * i + HALF * core, HALF), HALF), cols] = own[block, :] * (1.0 / TOTAL)
        gram[pl.ds(pl.multiple_of(CHANNELS * i + HALF * (1 - core), HALF), HALF), cols] = other[block, :] * (1.0 / TOTAL)
    above = lax.broadcasted_iota(jnp.int32, (128, 128), 1)
    below = lax.broadcasted_iota(jnp.int32, (128, 128), 0)
    for p in range(4):
        lo, hi = 128 * p, 128 * p + 128
        work[:, 0:128] = gram[lo:hi, lo:hi]
        work[:, 128:256] = (above == below).astype(f32)
        factor_diag(work, rows)
        upper[lo:hi, lo:hi] = jnp.where(above >= below, rows[:, 0:128], 0.0)
        if p > 0:
            upper[lo:hi, 0:lo] = jnp.zeros((128, lo), f32)
        inverse = jnp.where(above <= below, rows[:, 128:256], 0.0)
        stacked = triple(inverse, "hhl", 1)
        if p > 0:
            left = dot_nn(stacked, triple(behind[lo:hi, 0:lo], "hlh", 0))
            full = jnp.concatenate([left, inverse], axis=1)
        else:
            full = inverse
        if p < 3:
            right = dot_nn(stacked, triple(gram[lo:hi, hi:512], "hlh", 0))
            upper[lo:hi, hi:512] = right
            first, second = triple(right, "hhl", 0), triple(right, "hlh", 0)
            for q in range(p + 1, 4):
                a = 128 * (q - p - 1)
                at = slice(128 * q, 128 * q + 128), slice(128 * q, 512)
                gram[at] = gram[at] - dot_tn(first[:, a : a + 128], second[:, a:])
            change = dot_tn(first, triple(full, "hlh", 0))
            if p > 0:
                behind[hi:512, 0:lo] = behind[hi:512, 0:lo] - change[:, 0:lo]
            behind[hi:512, lo:hi] = -change[:, lo:hi]
        high, low = split(full)
        basis[:, lo:hi] = (dot_nt(hankel[:, 0:hi], high) + dot_nt(hankel[:, 0:hi], low)).astype(bf16)


def shards(records, dropout, counts):
    z = lax.axis_index("dev") // 2
    core = lax.axis_index("dev") % 2
    place = jnp.stack([z, core]).astype(jnp.int32)
    recs, drops = records.T, dropout.T
    head = (recs[:, :128].astype(f32) * drops[:, :128].astype(f32)).astype(bf16)
    head = lax.ppermute(head, "grp", [(g, g - 1) for g in range(1, GROUPS)])
    sent = pl.pallas_call(
        pack_kernel,
        out_shape=jax.ShapeDtypeStruct((32, 4, WINDOW), bf16),
        in_specs=[SMEM, VMEM, VMEM, VMEM],
        compiler_params=PARAMS,
        name="pack",
    )(counts, recs, drops, head)
    series = lax.all_to_all(sent, "dev", 0, 0, tiled=True).reshape(CHANNELS, WINDOW)
    packed, hankel = pl.pallas_call(
        gram_kernel,
        out_shape=(jax.ShapeDtypeStruct((PACKED, 128), f32), jax.ShapeDtypeStruct((ROWS, COLS), bf16)),
        in_specs=[SMEM, VMEM],
        scratch_shapes=[pltpu.VMEM((COLS, 512), bf16)],
        compiler_params=PARAMS,
        name="partial_gram",
    )(place, series)
    add = pl.pallas_call(
        sum_kernel,
        out_shape=jax.ShapeDtypeStruct((GROUPS, SLICE, 128), f32),
        compiler_params=PARAMS,
        name="add_up",
    )
    along_z = [[2 * a + c for a in range(16)] for c in range(2)]
    parts = lax.all_to_all(packed.reshape(GROUPS, SLICE, 128), "grp", 0, 0, tiled=True)
    parts = lax.all_to_all(add(parts), "dev", 0, 0, axis_index_groups=along_z, tiled=True)
    own = lax.all_to_all(add(parts), "grp", 0, 0, tiled=True).reshape(PACKED, 128)
    other = lax.ppermute(own, "dev", [(d, d ^ 1) for d in range(32)])
    upper, basis = pl.pallas_call(
        factor_kernel,
        out_shape=(jax.ShapeDtypeStruct((COLS, COLS), f32), jax.ShapeDtypeStruct((ROWS, COLS), bf16)),
        in_specs=[SMEM, VMEM, VMEM, VMEM],
        scratch_shapes=[
            pltpu.VMEM((COLS, COLS), f32),
            pltpu.VMEM((128, 256), f32),
            pltpu.VMEM((128, 256), f32),
            pltpu.VMEM((COLS, 384), f32),
        ],
        compiler_params=PARAMS,
        name="factor",
    )(place, own, other, hankel)
    return (upper, basis)


def solution(mesh):
    in_specs = (P("grp", "dev"), P("grp", "dev"), P(("grp", "dev")))
    out_specs = (P(), P(("grp", "dev"), None))
    return jax.shard_map(shards, mesh=mesh, in_specs=in_specs, out_specs=out_specs, check_vma=False)
```

time: 2020 us -> 129 us (0.06)
  local copies, waits for them, and re-layouts: 614 us -> 1.79 us
  other arithmetic: 489 us -> 0.78 us
  waiting for transfers between devices: 476 us -> 21.3 us
  loops' own time: 377 us -> 0 us
  blocking collectives: 0 us -> 45.5 us
  Pallas kernels: 0 us -> 27.9 us
    psum x1 -> x0, waiting for transfers between devices: 462 us -> none  [shards(): gram = lax.psum(partial_value, ('grp', 'dev'))]
    another operation x4 -> x0, loops' own time: 377 us -> none  [factor_block(): lax.fori_loop(0, size, eliminate, (augmented, jnp.zeros_like(augmented)))]
    mul x512 -> x0, other arithmetic: 337 us -> none  [eliminate(): working = working - factor[:, None] * pivot_row[None, :]]
    dynamic_update_slice x512 -> x0, local copies, waits for them, and re-layouts: 312 us -> none  [eliminate(): written = lax.dynamic_update_slice_in_dim(written, scaled[None, :], step, 0)]
    dynamic_slice x512 -> x0, local copies, waits for them, and re-layouts: 301 us -> none  [eliminate(): pivot = lax.dynamic_slice_in_dim(pivot_row, step, 1, 0)[0]]
    div x513 -> x0, other arithmetic: 95.9 us -> none  [the longest x512 94.6 us: eliminate(): scaled = pivot_row / jnp.sqrt(pivot)]
    sub x512 -> x0, other arithmetic: 53.9 us -> none  [eliminate(): working = working - factor[:, None] * pivot_row[None, :]]
    all_to_all x0 -> x3, blocking collectives: none -> 45.5 us  [the longest x1 18.5 us: shards(): lax.all_to_all(add(parts), 'dev', 0, 0, axis_index_groups=along_z, tiled=...]
where the time goes in v1:
time: 129 us; the launch traced here: 128 us
  blocking collectives  45.5 us (35%)
  starting transfers between devices  29.6 us (23%)
  Pallas kernels  27.9 us (22%)
  waiting for transfers between devices  21.3 us (17%)
  local copies, waits for them, and re-layouts  1.79 us (1%)
  between operations  1.34 us (1%)
    pallas_call x1, Pallas kernels, shards(): pl.pallas_call(factor_kernel, out_shape=(jax.ShapeDtypeStruct((COLS, COLS...  26.1 us
    all_to_all x1, blocking collectives, shards(): lax.all_to_all(add(parts), 'dev', 0, 0, axis_index_groups=along_z, tiled=...  18.5 us
    all_to_all x1, starting transfers between devices, shards(): lax.all_to_all(sent, 'dev', 0, 0, tiled=True).reshape(CHANNELS, WINDOW)  17.2 us
    all_to_all x1, waiting for transfers between devices, shards(): lax.all_to_all(sent, 'dev', 0, 0, tiled=True).reshape(CHANNELS, WINDOW)  17 us
    all_to_all x1, blocking collectives, shards(): lax.all_to_all(packed.reshape(GROUPS, SLICE, 128), 'grp', 0, 0, tiled=True)  16.2 us
    ppermute x1, starting transfers between devices, shards(): other = lax.ppermute(own, 'dev', [(d, d ^ 1) for d in range(32)])  11.1 us
    all_to_all x1, blocking collectives, shards(): lax.all_to_all(add(parts), 'grp', 0, 0, tiled=True).reshape(PACKED, 128)  10.8 us
    ppermute x1, waiting for transfers between devices, shards(): head = lax.ppermute(head, 'grp', [(g, g - 1) for g in range(1, GROUPS)])  3.04 us
  transfers between devices with their start and end apart: 3, of which 3 were waited for; matrix products, arithmetic and copies ran while one was open for 0% of the time, Pallas kernels for 0%

profile of v1, /device:TPU:1, one launch (start us, length us, event | category | flops | bytes accessed | tf_op | source)
XLA Modules:
  0.0 128.2 jit_solution(10549292934380791140)
XLA Ops:
  0.6 0.7 fusion.1
  1.3 1.3 collective-permute-start
  3.3 3.0 %collective-permute-done.head = bf16[4,128]{1,0:T(4,128)(2,1)S(1)} collective-permute-done((bf16[4,128]{1,0:T(4,128)(2,1)S(1)}, bf16[4,128]{1,0:T(4,128)(2,1)S(1)}, u32[]{:S(2)}, u32[]{:S(2)}) %collective-permute-start) | collective-permute-done | bytes 1056 | tf_op jit(solution)/shard_map/ppermute | solution.py:169
  6.3 0.0 copy-start
  6.3 0.9 copy-done
  7.2 0.0 copy-start.1
  7.2 0.8 copy-done.1
  8.1 0.7 pack.1
  8.8 17.2 %all-to-all-start = ((bf16[32,4,640]{2,1,0:T(4,128)(2,1)}), bf16[32,4,640]{2,1,0:T(4,128)(2,1)S(1)}, u32[]{:S(2)}, u32[]{:S(2)}) async-start(bf16[32,4,640]{2,1,0:T(4,128)(2,1)} %pack.1), calls=%async_computation | async-start | bytes 327680 | tf_op jit(solution)/shard_map/all_to_all | solution.py:177
  26.0 0.1 pad_add_fusion.place
  26.1 17.0 %all-to-all-done = bf16[32,4,640]{2,1,0:T(4,128)(2,1)S(1)} async-done(((bf16[32,4,640]{2,1,0:T(4,128)(2,1)}), bf16[32,4,640]{2,1,0:T(4,128)(2,1)S(1)}, u32[]{:S(2)}, u32[]{:S(2)}) %all-to-all-start) | async-done | bytes 163872 | tf_op jit(solution)/shard_map/all_to_all | solution.py:177
  43.2 1.0 partial_gram.1
  44.2 16.2 %all_to_all.20.parts = f32[16,40,128]{2,1,0:T(8,128)S(1)} all-to-all(f32[16,40,128]{2,1,0:T(8,128)S(1)} %bitcast.8), channel_id=1, replica_groups=mesh['grp'=16,'dev'=32] {'grp'}, dimensions={0} | all-to-all | bytes 655360 | tf_op jit(solution)/shard_map/all_to_all | solution.py:193
  60.4 18.5 %all_to_all.21.parts = f32[16,40,128]{2,1,0:T(8,128)S(1)} all-to-all(f32[16,40,128]{2,1,0:T(8,128)S(1)} %add_up.2), channel_id=1, replica_groups={{0,2,4,6,8,10,12,14,16,18,20,22,24,26,28,30},{1,3,5,7,9,11,13,15,17,19,..., dimensions={0} | all-to-all | bytes 655360 | tf_op jit(solution)/shard_map/all_to_all | solution.py:194
  79.0 10.8 %all_to_all.22 = f32[16,40,128]{2,1,0:T(8,128)S(1)} all-to-all(f32[16,40,128]{2,1,0:T(8,128)S(1)} %add_up.3), channel_id=1, replica_groups=mesh['grp'=16,'dev'=32] {'grp'}, dimensions={0} | all-to-all | bytes 655360 | tf_op jit(solution)/shard_map/all_to_all | solution.py:195
  89.8 11.1 %collective-permute-start.1 = (f32[640,128]{1,0:T(8,128)S(1)}, f32[640,128]{1,0:T(8,128)S(1)}, u32[]{:S(2)}, u32[]{:S(2)}) collective-permute-start(f32[640,128]{1,0:T(8,128)S(1)} %bitcast.6), channel_id=1, source_target_pairs={{0,1},{1,0},{2,3},{3,2},{4,5},{5,4},{6,7},{7,6},{8,9},{9,8},{10,11... | collective-permute-start | bytes 983048 | tf_op jit(solution)/shard_map/ppermute | solution.py:196
  100.8 1.2 collective-permute-done.1.other
  102.1 26.1 %factor.1 = (f32[512,512]{1,0:T(8,128)}, bf16[256,512]{1,0:T(8,128)(2,1)}) custom-call(s32[2]{0:T(128)S(1)} %pad_add_fusion.place, f32[640,128]{1,0:T(8,128)S(1)} %bitcast.7, f32[640,128]{1,0:T(8,128)S(1)} %collective-permute-done.1.other, bf16[256,512]{1,0:T(8,128)(2,1)S(1)} %get-tuple-element.5.hankel), custom_call_target="tpu_custom_call" | custom-call | tf_op jit(solution)/shard_map/factor/pallas_call | solution.py:197
  (3 shorter events, 0.1 us)
Async XLA Ops:
  1.3 5.0 %collective-permute-start = (bf16[4,128]{1,0:T(4,128)(2,1)S(1)}, bf16[4,128]{1,0:T(4,128)(2,1)S(1)}, u32[]{:S(2)}, u32[]{:S(2)}) collective-permute-start(bf16[4,128]{1,0:T(4,128)(2,1)S(1)} %fusion.1), channel_id=1, source_target_pairs={{32,0},{64,32},{96,64},{128,96},{160,128},{192,160},{224,192},{256... | collective-permute-start | bytes 3080 | tf_op jit(solution)/shard_map/ppermute | solution.py:169
  6.3 0.9 copy-start
  7.2 0.8 copy-start.1
  8.8 34.4 %all-to-all-start = ((bf16[32,4,640]{2,1,0:T(4,128)(2,1)}), bf16[32,4,640]{2,1,0:T(4,128)(2,1)S(1)}, u32[]{:S(2)}, u32[]{:S(2)}) async-start(bf16[32,4,640]{2,1,0:T(4,128)(2,1)} %pack.1), calls=%async_computation | async-start | bytes 327680 | tf_op jit(solution)/shard_map/all_to_all | solution.py:177
  89.8 12.3 %collective-permute-start.1 = (f32[640,128]{1,0:T(8,128)S(1)}, f32[640,128]{1,0:T(8,128)S(1)}, u32[]{:S(2)}, u32[]{:S(2)}) collective-permute-start(f32[640,128]{1,0:T(8,128)S(1)} %bitcast.6), channel_id=1, source_target_pairs={{0,1},{1,0},{2,3},{3,2},{4,5},{5,4},{6,7},{7,6},{8,9},{9,8},{10,11... | collective-permute-start | bytes 983048 | tf_op jit(solution)/shard_map/ppermute | solution.py:196

commit v2 on v1

v2 whole, which is shorter than its diff:
```python
import jax
import jax.numpy as jnp
from jax import lax
from jax.experimental import pallas as pl
from jax.experimental.pallas import tpu as pltpu
from jax.sharding import Mesh
from jax.sharding import PartitionSpec as P

f32, bf16 = jnp.float32, jnp.bfloat16

LAGS = 4
CHANNELS = 128
ROWS = 256
COLS = 512
TOTAL = 131072
GROUPS = 16
OWNERS = 32
PLANES = 8
WINDOW = 640
PAIRS = [(i, j) for i in range(LAGS) for j in range(i, LAGS)]
HALF = 64
SLICE = HALF * len(PAIRS) // OWNERS
STEP = 32

PARAMS = pltpu.CompilerParams(vmem_limit_bytes=48 * 2**20)
SMEM = pl.BlockSpec(memory_space=pltpu.SMEM)
VMEM = pl.BlockSpec(memory_space=pltpu.VMEM)
ANY = pl.BlockSpec(memory_space=pl.ANY)


def split(x):
    high = x.astype(bf16)
    return high, (x - high.astype(f32)).astype(bf16)


def dot_tn(left, right):
    return lax.dot_general(left, right, (((0,), (0,)), ((), ())), preferred_element_type=f32)


def dot_nt(left, right):
    return lax.dot_general(left, right, (((1,), (1,)), ((), ())), preferred_element_type=f32)


def dot_nn(left, right):
    return jnp.dot(left, right, preferred_element_type=f32)


def triple(x, order, axis):
    high, low = split(x)
    return jnp.concatenate([low if c == "l" else high for c in order], axis=axis)


def pack_kernel(place, count, records, dropout, out):
    signal = (records[...].astype(f32) * dropout[...].astype(f32)).astype(bf16)
    lane = lax.broadcasted_iota(jnp.int32, (4, 128), 1)
    counted = jnp.full((4, 128), count[0], jnp.int32).astype(f32)
    for z in range(16):
        behind = signal[:, 512 * z + 512 : 512 * z + 640] if z < 15 else jnp.zeros((4, 128), bf16)
        behind = jnp.where(lane == 127, counted, behind.astype(f32)).astype(bf16)
        for core in range(2):
            out[2 * z + core, :, 0:512] = signal[:, 512 * z : 512 * z + 512]
            out[2 * z + core, :, 512:640] = behind


def head_kernel(count, head, packed, out, behind, sem):
    lane = lax.broadcasted_iota(jnp.int32, (4, 128), 1)
    counted = jnp.full((4, 128), count[0], jnp.int32).astype(f32)
    value = jnp.where(lane == 127, counted, head[...].astype(f32)).astype(bf16)
    behind[0] = value
    behind[1] = value
    copy = pltpu.make_async_copy(behind, out.at[30:32, :, 512:640], sem)
    copy.start()
    copy.wait()


def gram_kernel(place, series, packed, hankel, lagged):
    z, core = place[0], place[1]
    samples = series[...].astype(f32)
    source = lax.broadcasted_iota(jnp.int32, (CHANNELS, 1), 0)
    tail = samples[:, WINDOW - 1 : WINDOW]
    time = lax.broadcasted_iota(jnp.int32, (1, 512), 1)
    counts = [
        jnp.sum(jnp.where(source == 8 * z + 4 * e, tail, 0.0), axis=0, keepdims=True) for e in range(2)
    ]
    least = jnp.where(time < ROWS, ROWS - counts[0], 2 * ROWS - counts[1])
    valid = time.astype(f32) >= least
    for i in range(LAGS):
        moved = samples if i == 0 else pltpu.roll(samples, WINDOW - i, 1)
        lagged[CHANNELS * i : CHANNELS * (i + 1), :] = jnp.where(valid, moved[:, :512], 0.0).astype(bf16)
    every = lagged[...]
    mine = jnp.concatenate(
        [lagged[pl.ds(pl.multiple_of(CHANNELS * i + HALF * core, HALF), HALF), :] for i in range(LAGS)], axis=0
    )
    gram = dot_nt(mine, every)

    def tile(t):
        (i, j), s = PAIRS[t // 8], t % 8
        return gram[HALF * i + 8 * s : HALF * i + 8 * s + 8, CHANNELS * j : CHANNELS * (j + 1)]

    for m in range(OWNERS):
        packed[m, 0:8, :] = tile(2 * m)
        packed[m, 8:16, :] = tile(2 * m + 1)
        packed[m, 16:20, :] = tile(2 * OWNERS + m // 2)[4 * (m % 2) : 4 * (m % 2) + 4, :]
    own = lagged[:, pl.ds(pl.multiple_of(ROWS * core, ROWS), ROWS)]
    hankel[...] = jnp.transpose(own.astype(f32)).astype(bf16)


def sum_kernel(parts, out):
    total = parts[0]
    for s in range(1, parts.shape[0]):
        total = total + parts[s]
    for s in range(out.shape[0]):
        out[s] = total


def add_up(parts, copies):
    return pl.pallas_call(
        sum_kernel,
        out_shape=jax.ShapeDtypeStruct((copies, SLICE, 128), f32),
        compiler_params=PARAMS,
        name="add_up",
    )(parts)


def spread(value, sublane):
    return jnp.broadcast_to(value[sublane : sublane + 1, :], (8, 128))


def pivots(work, start):
    sub = lax.broadcasted_iota(jnp.int32, (8, 128), 0)
    blocks = STEP // 8
    parts = [
        [work[start + 8 * b : start + 8 * b + 8, 128 * t : 128 * t + 128] for t in range(2)] for b in range(blocks)
    ]
    cols = [
        {b: jnp.broadcast_to(parts[b][0][:, start + i : start + i + 1], (8, 128)) for b in range(i // 8, blocks)}
        for i in range(STEP)
    ]
    scale = [jnp.ones((8, 128), f32) for b in range(blocks)]
    for k in range(STEP):
        at, ks = k // 8, k % 8
        pivot = spread(cols[k][at], ks)
        inverse = 1.0 / pivot
        factor = {b: cols[k][b] * inverse for b in range(at, blocks)}
        scale[at] = jnp.where(sub == ks, lax.rsqrt(pivot), scale[at])
        for i in range(k + 1, STEP):
            beside = spread(cols[k][i // 8], i % 8)
            for b in range(i // 8, blocks):
                cols[i][b] = cols[i][b] - factor[b] * beside
        factor[at] = jnp.where(sub > ks, factor[at], 0.0)
        for t in range(2):
            row = spread(parts[at][t], ks)
            for b in range(at, blocks):
                parts[b][t] = parts[b][t] - factor[b] * row
    return jnp.concatenate(
        [jnp.concatenate([parts[b][t] * scale[b] for t in range(2)], axis=1) for b in range(blocks)], axis=0
    )


def factor_diag(work, rows):
    for start in range(0, 128, STEP):
        after = start + STEP
        done = pivots(work, start)
        rows[start:after, :] = done
        if after < 128:
            change = dot_tn(triple(done[:, :128], "hhl", 0), triple(done, "hlh", 0))
            work[after:128, :] = work[after:128, :] - change[after:128, :]


def factor_kernel(place, own, other, hankel, upper, basis, gram, work, rows, behind):
    core = place[1]
    for source, half in ((own, core), (other, 1 - core)):
        for t in range(2 * OWNERS + GROUPS):
            (i, j), s = PAIRS[t // 8], t % 8
            if t < 2 * OWNERS:
                value = source[t // 2, 8 * (t % 2) : 8 * (t % 2) + 8, :]
            else:
                m = 2 * (t - 2 * OWNERS)
                value = jnp.concatenate([source[m, 16:20, :], source[m + 1, 16:20, :]], axis=0)
            at = pl.multiple_of(CHANNELS * i + HALF * half + 8 * s, 8)
            gram[pl.ds(at, 8), CHANNELS * j : CHANNELS * (j + 1)] = value * (1.0 / TOTAL)
    above = lax.broadcasted_iota(jnp.int32, (128, 128), 1)
    below = lax.broadcasted_iota(jnp.int32, (128, 128), 0)
    for p in range(4):
        lo, hi = 128 * p, 128 * p + 128
        work[:, 0:128] = gram[lo:hi, lo:hi]
        work[:, 128:256] = (above == below).astype(f32)
        factor_diag(work, rows)
        upper[lo:hi, lo:hi] = jnp.where(above >= below, rows[:, 0:128], 0.0)
        if p > 0:
            upper[lo:hi, 0:lo] = jnp.zeros((128, lo), f32)
        inverse = jnp.where(above <= below, rows[:, 128:256], 0.0)
        stacked = triple(inverse, "hhl", 1)
        if p > 0:
            left = dot_nn(stacked, triple(behind[lo:hi, 0:lo], "hlh", 0))
            full = jnp.concatenate([left, inverse], axis=1)
        else:
            full = inverse
        if p < 3:
            right = dot_nn(stacked, triple(gram[lo:hi, hi:512], "hlh", 0))
            upper[lo:hi, hi:512] = right
            first, second = triple(right, "hhl", 0), triple(right, "hlh", 0)
            for q in range(p + 1, 4):
                a = 128 * (q - p - 1)
                at = slice(128 * q, 128 * q + 128), slice(128 * q, 512)
                gram[at] = gram[at] - dot_tn(first[:, a : a + 128], second[:, a:])
            change = dot_tn(first, triple(full, "hlh", 0))
            if p > 0:
                behind[hi:512, 0:lo] = behind[hi:512, 0:lo] - change[:, 0:lo]
            behind[hi:512, lo:hi] = -change[:, lo:hi]
        high, low = split(full)
        basis[:, lo:hi] = (dot_nt(hankel[:, 0:hi], high) + dot_nt(hankel[:, 0:hi], low)).astype(bf16)


def factor(place, own, other, hankel):
    return pl.pallas_call(
        factor_kernel,
        out_shape=(jax.ShapeDtypeStruct((COLS, COLS), f32), jax.ShapeDtypeStruct((ROWS, COLS), bf16)),
        in_specs=[SMEM, VMEM, VMEM, VMEM],
        scratch_shapes=[
            pltpu.VMEM((COLS, COLS), f32),
            pltpu.VMEM((128, 256), f32),
            pltpu.VMEM((128, 256), f32),
            pltpu.VMEM((COLS, 384), f32),
        ],
        compiler_params=PARAMS,
        name="factor",
    )(place, own, other, hankel)


def shards(records, dropout, counts):
    core = lax.axis_index("core")
    place = jnp.stack([2 * lax.axis_index("zh") + lax.axis_index("zl"), core]).astype(jnp.int32)
    recs, drops = records.T, dropout.T
    head = (recs[:, :128].astype(f32) * drops[:, :128].astype(f32)).astype(bf16)
    head = lax.ppermute(head, GRP, [(g, g - 1) for g in range(1, GROUPS)])
    sent = pl.pallas_call(
        pack_kernel,
        out_shape=jax.ShapeDtypeStruct((32, 4, WINDOW), bf16),
        in_specs=[SMEM, SMEM, VMEM, VMEM],
        compiler_params=PARAMS,
        cost_estimate=pl.CostEstimate(flops=10**5, bytes_accessed=10**6, transcendentals=0),
        name="pack",
    )(place, counts, recs, drops)
    sent = pl.pallas_call(
        head_kernel,
        out_shape=jax.ShapeDtypeStruct((32, 4, WINDOW), bf16),
        in_specs=[SMEM, VMEM, ANY],
        out_specs=ANY,
        input_output_aliases={2: 0},
        scratch_shapes=[pltpu.VMEM((2, 4, 128), bf16), pltpu.SemaphoreType.DMA],
        compiler_params=PARAMS,
        name="add_head",
    )(counts, head, sent)
    series = lax.all_to_all(sent, DEV, 0, 0, tiled=True).reshape(CHANNELS, WINDOW)
    packed, hankel = pl.pallas_call(
        gram_kernel,
        out_shape=(jax.ShapeDtypeStruct((OWNERS, SLICE, 128), f32), jax.ShapeDtypeStruct((ROWS, COLS), bf16)),
        in_specs=[SMEM, VMEM],
        scratch_shapes=[pltpu.VMEM((COLS, 512), bf16)],
        compiler_params=PARAMS,
        name="partial_gram",
    )(place, series)
    parts = lax.all_to_all(packed, OWNER, 0, 0, tiled=True)
    parts = lax.all_to_all(add_up(parts, PLANES), "zh", 0, 0, tiled=True)
    own = lax.all_to_all(add_up(parts, OWNERS), OWNER, 0, 0, tiled=True)
    other = lax.ppermute(own, "core", [(0, 1), (1, 0)])
    return factor(place, own, other, hankel)


GRP, DEV, OWNER = ("x", "y"), ("zh", "zl", "core"), ("x", "y", "zl")


def solution(mesh):
    fine = Mesh(mesh.devices.reshape(4, 4, PLANES, 2, 2), ("x", "y", "zh", "zl", "core"))
    in_specs = (P(GRP, DEV), P(GRP, DEV), P(GRP + DEV))
    out_specs = (P(), P(GRP + DEV, None))
    return jax.shard_map(shards, mesh=fine, in_specs=in_specs, out_specs=out_specs, check_vma=False)
```

time: 129 us -> 112 us (0.87)
  blocking collectives: 45.5 us -> 80.8 us
  starting transfers between devices: 29.6 us -> 8.19 us
  waiting for transfers between devices: 21.3 us -> 1.77 us
  Pallas kernels: 27.9 us -> 17.4 us
    all_to_all x3 -> x4, blocking collectives: 45.5 us -> 80.8 us  [the longest x1 34.2 us: shards(): lax.all_to_all(sent, DEV, 0, 0, tiled=True).reshape(CHANNELS, WINDOW)]
    all_to_all x1 -> x0, starting transfers between devices: 17.2 us -> none  [shards(): lax.all_to_all(sent, 'dev', 0, 0, tiled=True).reshape(CHANNELS, WINDOW)]
    all_to_all x1 -> x0, waiting for transfers between devices: 17 us -> none  [shards(): lax.all_to_all(sent, 'dev', 0, 0, tiled=True).reshape(CHANNELS, WINDOW)]
    pallas_call x4 -> x5, Pallas kernels: 27.2 us -> 16.8 us  [the longest x1 15.6 us: factor(): pl.pallas_call(factor_kernel, out_shape=(jax.ShapeDtypeStruct((COLS, COLS...]
    ppermute x2, starting transfers between devices: 12.3 us -> 8.19 us  [the longest x1 6.91 us: shards(): other = lax.ppermute(own, 'core', [(0, 1), (1, 0)])]
    ppermute x2, waiting for transfers between devices: 4.27 us -> 1.77 us  [the longest x1 1.15 us: shards(): other = lax.ppermute(own, 'core', [(0, 1), (1, 0)])]
  transfers between devices with their start and end apart: 3 -> 2, of which waited for: 3 -> 2; matrix products, arithmetic and copies ran while one was open for 0% -> 0% of each run, Pallas kernels for 0% -> 1%
where the time goes in v2:
time: 112 us
  blocking collectives  80.8 us (72%)
  Pallas kernels  17.4 us (16%)
  starting transfers between devices  8.19 us (7%)
  local copies, waits for them, and re-layouts  1.78 us (2%)
  waiting for transfers between devices  1.77 us (2%)
  between operations  1.35 us (1%)
    all_to_all x1, blocking collectives, shards(): lax.all_to_all(sent, DEV, 0, 0, tiled=True).reshape(CHANNELS, WINDOW)  34.2 us
    all_to_all x1, blocking collectives, shards(): parts = lax.all_to_all(packed, OWNER, 0, 0, tiled=True)  17.9 us
    all_to_all x1, blocking collectives, shards(): parts = lax.all_to_all(add_up(parts, PLANES), 'zh', 0, 0, tiled=True)  16.6 us
    pallas_call x1, Pallas kernels, factor(): pl.pallas_call(factor_kernel, out_shape=(jax.ShapeDtypeStruct((COLS, COLS...  15.6 us
    all_to_all x1, blocking collectives, shards(): own = lax.all_to_all(add_up(parts, OWNERS), OWNER, 0, 0, tiled=True)  12.1 us
    ppermute x1, starting transfers between devices, shards(): other = lax.ppermute(own, 'core', [(0, 1), (1, 0)])  6.91 us
  transfers between devices with their start and end apart: 2, of which 2 were waited for; matrix products, arithmetic and copies ran while one was open for 0% of the time, Pallas kernels for 1%

profile of v2, /device:TPU:1, one launch (start us, length us, event | category | flops | bytes accessed | tf_op | source)
XLA Modules:
  0.0 112.0 jit_solution(10529740003700500423)
XLA Ops:
  0.6 0.7 fusion.1
  1.3 1.3 %collective-permute-start = (bf16[4,128]{1,0:T(4,128)(2,1)S(1)}, bf16[4,128]{1,0:T(4,128)(2,1)S(1)}, u32[]{:S(2)}, u32[]{:S(2)}) collective-permute-start(bf16[4,128]{1,0:T(4,128)(2,1)S(1)} %fusion.1), channel_id=1, source_target_pairs={{32,0},{64,32},{96,64},{128,96},{160,128},{192,160},{224,192},{256... | collective-permute-start | bytes 3080 | tf_op jit(solution)/shard_map/ppermute | solution.py:236
  2.6 0.1 pad_add_fusion.place
  3.4 0.0 copy-start
  3.4 0.9 copy-done
  4.3 0.0 copy-start.1
  4.3 0.8 copy-done.1
  5.1 0.6 pack.1.packed
  5.7 0.6 collective-permute-done.head
  6.3 34.2 %all_to_all.20 = bf16[32,4,640]{2,1,0:T(4,128)(2,1)S(1)} all-to-all(bf16[32,4,640]{2,1,0:T(4,128)(2,1)S(1)} %add_head.1), channel_id=1, replica_groups=mesh['x'=4,'y'=4,'zh'=8,'zl'=2,'core'=2] {'zh','zl','core'}, dimensions={0} | all-to-all | bytes 327680 | tf_op jit(solution)/shard_map/all_to_all | solution.py:255
  40.6 1.0 partial_gram.1
  41.6 17.9 %all_to_all.21.parts = f32[32,20,128]{2,1,0:T(8,128)S(1)} all-to-all(f32[32,20,128]{2,1,0:T(8,128)S(1)} %get-tuple-element.4), channel_id=1, replica_groups=mesh['x'=4,'y'=4,'zh'=8,'zl'=2,'core'=2] {'x','y','zl'}, dimensions={0} | all-to-all | bytes 655360 | tf_op jit(solution)/shard_map/all_to_all | solution.py:264
  59.6 16.6 %all_to_all.22.parts = f32[8,20,128]{2,1,0:T(8,128)S(1)} all-to-all(f32[8,20,128]{2,1,0:T(8,128)S(1)} %add_up.2), channel_id=1, replica_groups=mesh['x'=4,'y'=4,'zh'=8,'zl'=2,'core'=2] {'zh'}, dimensions={0} | all-to-all | bytes 163840 | tf_op jit(solution)/shard_map/all_to_all | solution.py:265
  76.2 12.1 %all_to_all.23.own = f32[32,20,128]{2,1,0:T(8,128)S(1)} all-to-all(f32[32,20,128]{2,1,0:T(8,128)S(1)} %add_up.3), channel_id=1, replica_groups=mesh['x'=4,'y'=4,'zh'=8,'zl'=2,'core'=2] {'x','y','zl'}, dimensions={0} | all-to-all | bytes 655360 | tf_op jit(solution)/shard_map/all_to_all | solution.py:266
  88.3 6.9 %collective-permute-start.1 = (f32[32,20,128]{2,1,0:T(8,128)S(1)}, f32[32,20,128]{2,1,0:T(8,128)S(1)}, u32[]{:S(2)}, u32[]{:S(2)}) collective-permute-start(f32[32,20,128]{2,1,0:T(8,128)S(1)} %all_to_all.23.own), channel_id=1, source_target_pairs={{0,1},{1,0},{2,3},{3,2},{4,5},{5,4},{6,7},{7,6},{8,9},{9,8},{10,11... | collective-permute-start | bytes 983048 | tf_op jit(solution)/shard_map/ppermute | solution.py:267
  95.2 1.1 %collective-permute-done.1.other = f32[32,20,128]{2,1,0:T(8,128)S(1)} collective-permute-done((f32[32,20,128]{2,1,0:T(8,128)S(1)}, f32[32,20,128]{2,1,0:T(8,128)S(1)}, u32[]{:S(2)}, u32[]{:S(2)}) %collective-permute-start.1) | collective-permute-done | bytes 327712 | tf_op jit(solution)/shard_map/ppermute | solution.py:267
  96.3 15.6 %factor.1 = (f32[512,512]{1,0:T(8,128)}, bf16[256,512]{1,0:T(8,128)(2,1)}) custom-call(s32[2]{0:T(128)S(1)} %pad_add_fusion.place, f32[32,20,128]{2,1,0:T(8,128)S(1)} %all_to_all.23.own, f32[32,20,128]{2,1,0:T(8,128)S(1)} %collective-permute-done.1.other, bf16[256,512]{1,0:T(8,128)(2,1)S(1)} %get-tuple-element.5.hankel), custom_call_target="tpu_custom_call" | custom-call | tf_op jit(solution)/shard_map/factor/pallas_call | solution.py:216
  (4 shorter events, 0.1 us)
Async XLA Ops:
  1.3 5.0 %collective-permute-start = (bf16[4,128]{1,0:T(4,128)(2,1)S(1)}, bf16[4,128]{1,0:T(4,128)(2,1)S(1)}, u32[]{:S(2)}, u32[]{:S(2)}) collective-permute-start(bf16[4,128]{1,0:T(4,128)(2,1)S(1)} %fusion.1), channel_id=1, source_target_pairs={{32,0},{64,32},{96,64},{128,96},{160,128},{192,160},{224,192},{256... | collective-permute-start | bytes 3080 | tf_op jit(solution)/shard_map/ppermute | solution.py:236
  3.4 0.9 copy-start
  4.3 0.8 copy-start.1
  88.3 8.1 %collective-permute-start.1 = (f32[32,20,128]{2,1,0:T(8,128)S(1)}, f32[32,20,128]{2,1,0:T(8,128)S(1)}, u32[]{:S(2)}, u32[]{:S(2)}) collective-permute-start(f32[32,20,128]{2,1,0:T(8,128)S(1)} %all_to_all.23.own), channel_id=1, source_target_pairs={{0,1},{1,0},{2,3},{3,2},{4,5},{5,4},{6,7},{7,6},{8,9},{9,8},{10,11... | collective-permute-start | bytes 983048 | tf_op jit(solution)/shard_map/ppermute | solution.py:267

commit v3 on v2

--- a/solution.py
+++ b/solution.py
@@ -20,12 +20,14 @@
 PAIRS = [(i, j) for i in range(LAGS) for j in range(i, LAGS)]
 HALF = 64
 SLICE = HALF * len(PAIRS) // OWNERS
+TALL = SLICE + 4
+EDGE = 48
+INNER = 16
 STEP = 32
 
 PARAMS = pltpu.CompilerParams(vmem_limit_bytes=48 * 2**20)
 SMEM = pl.BlockSpec(memory_space=pltpu.SMEM)
 VMEM = pl.BlockSpec(memory_space=pltpu.VMEM)
-ANY = pl.BlockSpec(memory_space=pl.ANY)
 
 
 def split(x):
@@ -62,18 +64,7 @@
             out[2 * z + core, :, 512:640] = behind
 
 
-def head_kernel(count, head, packed, out, behind, sem):
-    lane = lax.broadcasted_iota(jnp.int32, (4, 128), 1)
-    counted = jnp.full((4, 128), count[0], jnp.int32).astype(f32)
-    value = jnp.where(lane == 127, counted, head[...].astype(f32)).astype(bf16)
-    behind[0] = value
-    behind[1] = value
-    copy = pltpu.make_async_copy(behind, out.at[30:32, :, 512:640], sem)
-    copy.start()
-    copy.wait()
-
-
-def gram_kernel(place, series, packed, hankel, lagged):
+def gram_kernel(place, series, packed, hankel, edge, lagged):
     z, core = place[0], place[1]
     samples = series[...].astype(f32)
     source = lax.broadcasted_iota(jnp.int32, (CHANNELS, 1), 0)
@@ -83,7 +74,8 @@
         jnp.sum(jnp.where(source == 8 * z + 4 * e, tail, 0.0), axis=0, keepdims=True) for e in range(2)
     ]
     least = jnp.where(time < ROWS, ROWS - counts[0], 2 * ROWS - counts[1])
-    valid = time.astype(f32) >= least
+    own_rows = jnp.where(z == 15, 2 * ROWS - 3, 2 * ROWS)
+    valid = (time.astype(f32) >= least) & (time < own_rows)
     for i in range(LAGS):
         moved = samples if i == 0 else pltpu.roll(samples, WINDOW - i, 1)
         lagged[CHANNELS * i : CHANNELS * (i + 1), :] = jnp.where(valid, moved[:, :512], 0.0).astype(bf16)
@@ -103,23 +95,27 @@
         packed[m, 16:20, :] = tile(2 * OWNERS + m // 2)[4 * (m % 2) : 4 * (m % 2) + 4, :]
     own = lagged[:, pl.ds(pl.multiple_of(ROWS * core, ROWS), ROWS)]
     hankel[...] = jnp.transpose(own.astype(f32)).astype(bf16)
+    head = jnp.transpose(samples[:, 0:128])[0:8, :]
+    tail = pltpu.roll(jnp.transpose(samples[:, 384:512])[120:128, :], 3, 0)
+    used = lax.broadcasted_iota(jnp.int32, (8, 128), 0) < 3
+    edge[...] = jnp.where(used & (z == 0), head, 0.0) + jnp.where(used & (z == 15), tail, 0.0)
+
+
+def sum_edge_kernel(parts, edge, out):
+    total = parts[0]
+    for s in range(1, OWNERS):
+        total = total + parts[s]
+    for s in range(PLANES):
+        out[s, 0:SLICE, :] = total
+        out[s, SLICE:TALL, :] = edge[0:4, :]
 
 
 def sum_kernel(parts, out):
     total = parts[0]
-    for s in range(1, parts.shape[0]):
+    for s in range(1, PLANES):
         total = total + parts[s]
-    for s in range(out.shape[0]):
+    for s in range(OWNERS):
         out[s] = total
-
-
-def add_up(parts, copies):
-    return pl.pallas_call(
-        sum_kernel,
-        out_shape=jax.ShapeDtypeStruct((copies, SLICE, 128), f32),
-        compiler_params=PARAMS,
-        name="add_up",
-    )(parts)
 
 
 def spread(value, sublane):
@@ -132,18 +128,19 @@
     parts = [
         [work[start + 8 * b : start + 8 * b + 8, 128 * t : 128 * t + 128] for t in range(2)] for b in range(blocks)
     ]
-    cols = [
-        {b: jnp.broadcast_to(parts[b][0][:, start + i : start + i + 1], (8, 128)) for b in range(i // 8, blocks)}
-        for i in range(STEP)
-    ]
+    cols = {}
     scale = [jnp.ones((8, 128), f32) for b in range(blocks)]
     for k in range(STEP):
         at, ks = k // 8, k % 8
+        if k % INNER == 0:
+            for i in range(k, k + INNER):
+                lane = start + i
+                cols[i] = {b: jnp.broadcast_to(parts[b][0][:, lane : lane + 1], (8, 128)) for b in range(i // 8, blocks)}
         pivot = spread(cols[k][at], ks)
         inverse = 1.0 / pivot
         factor = {b: cols[k][b] * inverse for b in range(at, blocks)}
         scale[at] = jnp.where(sub == ks, lax.rsqrt(pivot), scale[at])
-        for i in range(k + 1, STEP):
+        for i in range(k + 1, k // INNER * INNER + INNER):
             beside = spread(cols[k][i // 8], i % 8)
             for b in range(i // 8, blocks):
                 cols[i][b] = cols[i][b] - factor[b] * beside
@@ -167,8 +164,31 @@
             work[after:128, :] = work[after:128, :] - change[after:128, :]
 
 
-def factor_kernel(place, own, other, hankel, upper, basis, gram, work, rows, behind):
-    core = place[1]
+def edge_rows(own, samples):
+    for m in range(OWNERS):
+        samples[4 * m : 4 * m + 4, :] = own[m, SLICE:TALL, :]
+    known = samples[...].astype(bf16)
+    row = lax.broadcasted_iota(jnp.int32, (EDGE, 128), 0)
+    source = lax.broadcasted_iota(jnp.int32, (EDGE, 128), 1)
+    group = row % GROUPS
+    lags = []
+    for i in range(LAGS):
+        ahead = row // GROUPS + i
+        inside = (ahead < 3) & (source == 8 * group + 4 + ahead)
+        outside = (ahead >= 3) & (group < GROUPS - 1) & (source == 8 * group + 8 + ahead - 3)
+        lags.append(dot_nn((inside | outside).astype(f32).astype(bf16), known))
+    return jnp.concatenate(lags, axis=1).astype(bf16)
+
+
+def factor_kernel(place, own, other, hankel_in, upper, basis, gram, work, rows, behind, samples, hankel):
+    z, core, group = place[0], place[1], place[2]
+    edges = edge_rows(own, samples)
+    hankel[...] = hankel_in[...]
+    row = lax.broadcasted_iota(jnp.int32, (16, EDGE), 0)
+    taken = lax.broadcasted_iota(jnp.int32, (16, EDGE), 1)
+    ends = (row >= 13) & (taken == GROUPS * (row - 13) + group) & (z == 15) & (core == 1)
+    patch = dot_nn(ends.astype(f32).astype(bf16), edges)
+    hankel[240:256, :] = (hankel_in[240:256, :].astype(f32) + patch).astype(bf16)
     for source, half in ((own, core), (other, 1 - core)):
         for t in range(2 * OWNERS + GROUPS):
             (i, j), s = PAIRS[t // 8], t % 8
@@ -179,6 +199,9 @@
                 value = jnp.concatenate([source[m, 16:20, :], source[m + 1, 16:20, :]], axis=0)
             at = pl.multiple_of(CHANNELS * i + HALF * half + 8 * s, 8)
             gram[pl.ds(at, 8), CHANNELS * j : CHANNELS * (j + 1)] = value * (1.0 / TOTAL)
+    for i in range(LAGS):
+        at = slice(CHANNELS * i, CHANNELS * (i + 1)), slice(CHANNELS * i, COLS)
+        gram[at] = gram[at] + dot_tn(edges[:, at[0]], edges[:, at[1]]) * (1.0 / TOTAL)
     above = lax.broadcasted_iota(jnp.int32, (128, 128), 1)
     below = lax.broadcasted_iota(jnp.int32, (128, 128), 0)
     for p in range(4):
@@ -222,48 +245,44 @@
             pltpu.VMEM((128, 256), f32),
             pltpu.VMEM((128, 256), f32),
             pltpu.VMEM((COLS, 384), f32),
+            pltpu.VMEM((4 * OWNERS, 128), f32),
+            pltpu.VMEM((ROWS, COLS), bf16),
         ],
         compiler_params=PARAMS,
         name="factor",
     )(place, own, other, hankel)
 
 
+def call(kernel, out_shape, in_specs, name, scratch=()):
+    return pl.pallas_call(
+        kernel, out_shape=out_shape, in_specs=in_specs, scratch_shapes=scratch, compiler_params=PARAMS, name=name
+    )
+
+
 def shards(records, dropout, counts):
-    core = lax.axis_index("core")
-    place = jnp.stack([2 * lax.axis_index("zh") + lax.axis_index("zl"), core]).astype(jnp.int32)
-    recs, drops = records.T, dropout.T
-    head = (recs[:, :128].astype(f32) * drops[:, :128].astype(f32)).astype(bf16)
-    head = lax.ppermute(head, GRP, [(g, g - 1) for g in range(1, GROUPS)])
-    sent = pl.pallas_call(
-        pack_kernel,
-        out_shape=jax.ShapeDtypeStruct((32, 4, WINDOW), bf16),
-        in_specs=[SMEM, SMEM, VMEM, VMEM],
-        compiler_params=PARAMS,
-        cost_estimate=pl.CostEstimate(flops=10**5, bytes_accessed=10**6, transcendentals=0),
-        name="pack",
-    )(place, counts, recs, drops)
-    sent = pl.pallas_call(
-        head_kernel,
-        out_shape=jax.ShapeDtypeStruct((32, 4, WINDOW), bf16),
-        in_specs=[SMEM, VMEM, ANY],
-        out_specs=ANY,
-        input_output_aliases={2: 0},
-        scratch_shapes=[pltpu.VMEM((2, 4, 128), bf16), pltpu.SemaphoreType.DMA],
-        compiler_params=PARAMS,
-        name="add_head",
-    )(counts, head, sent)
+    group = 4 * lax.axis_index("x") + lax.axis_index("y")
+    z = 2 * lax.axis_index("zh") + lax.axis_index("zl")
+    place = jnp.stack([z, lax.axis_index("core"), group]).astype(jnp.int32)
+    sent = call(
+        pack_kernel, jax.ShapeDtypeStruct((32, 4, WINDOW), bf16), [SMEM, SMEM, VMEM, VMEM], "pack"
+    )(place, counts, records.T, dropout.T)
     series = lax.all_to_all(sent, DEV, 0, 0, tiled=True).reshape(CHANNELS, WINDOW)
-    packed, hankel = pl.pallas_call(
+    packed, hankel, edge = call(
         gram_kernel,
-        out_shape=(jax.ShapeDtypeStruct((OWNERS, SLICE, 128), f32), jax.ShapeDtypeStruct((ROWS, COLS), bf16)),
-        in_specs=[SMEM, VMEM],
-        scratch_shapes=[pltpu.VMEM((COLS, 512), bf16)],
-        compiler_params=PARAMS,
-        name="partial_gram",
+        (
+            jax.ShapeDtypeStruct((OWNERS, SLICE, 128), f32),
+            jax.ShapeDtypeStruct((ROWS, COLS), bf16),
+            jax.ShapeDtypeStruct((8, 128), f32),
+        ),
+        [SMEM, VMEM],
+        "partial_gram",
+        [pltpu.VMEM((COLS, 512), bf16)],
     )(place, series)
     parts = lax.all_to_all(packed, OWNER, 0, 0, tiled=True)
-    parts = lax.all_to_all(add_up(parts, PLANES), "zh", 0, 0, tiled=True)
-    own = lax.all_to_all(add_up(parts, OWNERS), OWNER, 0, 0, tiled=True)
+    parts = call(sum_edge_kernel, jax.ShapeDtypeStruct((PLANES, TALL, 128), f32), [VMEM, VMEM], "add_owners")(parts, edge)
+    parts = lax.all_to_all(parts, "zh", 0, 0, tiled=True)
+    parts = call(sum_kernel, jax.ShapeDtypeStruct((OWNERS, TALL, 128), f32), [VMEM], "add_planes")(parts)
+    own = lax.all_to_all(parts, OWNER, 0, 0, tiled=True)
     other = lax.ppermute(own, "core", [(0, 1), (1, 0)])
     return factor(place, own, other, hankel)
 

time: 112 us -> 107 us (0.955)
  blocking collectives: 80.8 us -> 78.4 us
  starting transfers between devices: 8.19 us -> 6.73 us
    all_to_all x1, blocking collectives: 17.9 us -> 16 us  [shards(): parts = lax.all_to_all(packed, OWNER, 0, 0, tiled=True)]
    ppermute x1 -> x0, starting transfers between devices: 1.28 us -> none  [shards(): head = lax.ppermute(head, GRP, [(g, g - 1) for g in range(1, GROUPS)])]
  transfers between devices with their start and end apart: 2 -> 1, of which waited for: 2 -> 1; matrix products, arithmetic and copies ran while one was open for 0% -> 0% of each run, Pallas kernels for 1% -> 0%
where the time goes in v3:
time: 107 us; the launch traced here: 106 us
  blocking collectives  78.4 us (73%)
  Pallas kernels  16.6 us (16%)
  starting transfers between devices  6.73 us (6%)
  local copies, waits for them, and re-layouts  1.79 us (2%)
  waiting for transfers between devices  1.33 us (1%)
  between operations  1.32 us (1%)
    all_to_all x1, blocking collectives, shards(): lax.all_to_all(sent, DEV, 0, 0, tiled=True).reshape(CHANNELS, WINDOW)  33.7 us
    all_to_all x1, blocking collectives, shards(): parts = lax.all_to_all(parts, 'zh', 0, 0, tiled=True)  16.6 us
    all_to_all x1, blocking collectives, shards(): parts = lax.all_to_all(packed, OWNER, 0, 0, tiled=True)  16 us
    pallas_call x1, Pallas kernels, factor(): pl.pallas_call(factor_kernel, out_shape=(jax.ShapeDtypeStruct((COLS, COLS...  14.9 us
    all_to_all x1, blocking collectives, shards(): own = lax.all_to_all(parts, OWNER, 0, 0, tiled=True)  12.1 us
    ppermute x1, starting transfers between devices, shards(): other = lax.ppermute(own, 'core', [(0, 1), (1, 0)])  6.73 us
  transfers between devices with their start and end apart: 1, of which 1 were waited for; matrix products, arithmetic and copies ran while one was open for 0% of the time, Pallas kernels for 0%

profile of v3, /device:TPU:1, one launch (start us, length us, event | category | flops | bytes accessed | tf_op | source)
XLA Modules:
  0.0 106.2 jit_solution(2087973612717786244)
XLA Ops:
  1.3 0.1 pad_add_fusion.place
  1.4 0.0 copy-start
  1.4 0.9 copy-done
  2.3 0.0 copy-start.1
  2.3 0.8 copy-done.1
  3.1 0.6 pack.1
  3.7 33.7 %all_to_all.20 = bf16[32,4,640]{2,1,0:T(4,128)(2,1)S(1)} all-to-all(bf16[32,4,640]{2,1,0:T(4,128)(2,1)S(1)} %pack.1), channel_id=1, replica_groups=mesh['x'=4,'y'=4,'zh'=8,'zl'=2,'core'=2] {'zh','zl','core'}, dimensions={0} | all-to-all | bytes 327680 | tf_op jit(solution)/shard_map/all_to_all | solution.py:269
  37.4 1.1 partial_gram.1
  38.5 16.0 %all_to_all.21.parts = f32[32,20,128]{2,1,0:T(8,128)S(1)} all-to-all(f32[32,20,128]{2,1,0:T(8,128)S(1)} %get-tuple-element.5), channel_id=1, replica_groups=mesh['x'=4,'y'=4,'zh'=8,'zl'=2,'core'=2] {'x','y','zl'}, dimensions={0} | all-to-all | bytes 655360 | tf_op jit(solution)/shard_map/all_to_all | solution.py:281
  54.5 16.6 %all_to_all.22.parts = f32[8,24,128]{2,1,0:T(8,128)S(1)} all-to-all(f32[8,24,128]{2,1,0:T(8,128)S(1)} %add_owners.1), channel_id=1, replica_groups=mesh['x'=4,'y'=4,'zh'=8,'zl'=2,'core'=2] {'zh'}, dimensions={0} | all-to-all | bytes 196608 | tf_op jit(solution)/shard_map/all_to_all | solution.py:283
  71.2 12.1 %all_to_all.23.own = f32[32,24,128]{2,1,0:T(8,128)S(1)} all-to-all(f32[32,24,128]{2,1,0:T(8,128)S(1)} %add_planes.1), channel_id=1, replica_groups=mesh['x'=4,'y'=4,'zh'=8,'zl'=2,'core'=2] {'x','y','zl'}, dimensions={0} | all-to-all | bytes 786432 | tf_op jit(solution)/shard_map/all_to_all | solution.py:285
  83.2 6.7 %collective-permute-start = (f32[32,24,128]{2,1,0:T(8,128)S(1)}, f32[32,24,128]{2,1,0:T(8,128)S(1)}, u32[]{:S(2)}, u32[]{:S(2)}) collective-permute-start(f32[32,24,128]{2,1,0:T(8,128)S(1)} %all_to_all.23.own), channel_id=1, source_target_pairs={{0,1},{1,0},{2,3},{3,2},{4,5},{5,4},{6,7},{7,6},{8,9},{9,8},{10,11... | collective-permute-start | bytes 1179656 | tf_op jit(solution)/shard_map/ppermute | solution.py:286
  90.0 1.3 %collective-permute-done.other = f32[32,24,128]{2,1,0:T(8,128)S(1)} collective-permute-done((f32[32,24,128]{2,1,0:T(8,128)S(1)}, f32[32,24,128]{2,1,0:T(8,128)S(1)}, u32[]{:S(2)}, u32[]{:S(2)}) %collective-permute-start) | collective-permute-done | bytes 393248 | tf_op jit(solution)/shard_map/ppermute | solution.py:286
  91.3 14.9 %factor.1 = (f32[512,512]{1,0:T(8,128)}, bf16[256,512]{1,0:T(8,128)(2,1)}) custom-call(s32[3]{0:T(128)S(1)} %pad_add_fusion.place, f32[32,24,128]{2,1,0:T(8,128)S(1)} %all_to_all.23.own, f32[32,24,128]{2,1,0:T(8,128)S(1)} %collective-permute-done.other, bf16[256,512]{1,0:T(8,128)(2,1)S(1)} %get-tuple-element.7.hankel_in), custom_call_target="tpu_custom_call" | custom-call | tf_op jit(solution)/shard_map/factor/pallas_call | solution.py:239
  (3 shorter events, 0.1 us)
Async XLA Ops:
  1.4 0.9 copy-start
  2.3 0.8 copy-start.1
  83.2 8.1 %collective-permute-start = (f32[32,24,128]{2,1,0:T(8,128)S(1)}, f32[32,24,128]{2,1,0:T(8,128)S(1)}, u32[]{:S(2)}, u32[]{:S(2)}) collective-permute-start(f32[32,24,128]{2,1,0:T(8,128)S(1)} %all_to_all.23.own), channel_id=1, source_target_pairs={{0,1},{1,0},{2,3},{3,2},{4,5},{5,4},{6,7},{7,6},{8,9},{9,8},{10,11... | collective-permute-start | bytes 1179656 | tf_op jit(solution)/shard_map/ppermute | solution.py:286

commit v4 on v3

--- a/solution.py
+++ b/solution.py
@@ -23,6 +23,7 @@
 TALL = SLICE + 4
 EDGE = 48
 INNER = 16
+EARLY = 4
 STEP = 32
 
 PARAMS = pltpu.CompilerParams(vmem_limit_bytes=48 * 2**20)
@@ -124,44 +125,62 @@
 
 def pivots(work, start):
     sub = lax.broadcasted_iota(jnp.int32, (8, 128), 0)
+    lane = lax.broadcasted_iota(jnp.int32, (8, 128), 1)
     blocks = STEP // 8
-    parts = [
-        [work[start + 8 * b : start + 8 * b + 8, 128 * t : 128 * t + 128] for t in range(2)] for b in range(blocks)
-    ]
+    parts = [work[start + 8 * b : start + 8 * b + 8, :] for b in range(blocks)]
     cols = {}
     scale = [jnp.ones((8, 128), f32) for b in range(blocks)]
-    for k in range(STEP):
+    for k in range(0, STEP, 2):
         at, ks = k // 8, k % 8
-        if k % INNER == 0:
-            for i in range(k, k + INNER):
-                lane = start + i
-                cols[i] = {b: jnp.broadcast_to(parts[b][0][:, lane : lane + 1], (8, 128)) for b in range(i // 8, blocks)}
-        pivot = spread(cols[k][at], ks)
-        inverse = 1.0 / pivot
-        factor = {b: cols[k][b] * inverse for b in range(at, blocks)}
-        scale[at] = jnp.where(sub == ks, lax.rsqrt(pivot), scale[at])
-        for i in range(k + 1, k // INNER * INNER + INNER):
-            beside = spread(cols[k][i // 8], i % 8)
+        if k == 0 or k % INNER == INNER - EARLY:
+            for i in range(len(cols), min(len(cols) + INNER, STEP)):
+                c = start + i
+                cols[i] = {b: jnp.broadcast_to(parts[b][:, c : c + 1], (8, 128)) for b in range(i // 8, blocks)}
+        one, two = cols[k], cols[k + 1]
+        first, cross, second = spread(one[at], ks), spread(one[at], ks + 1), spread(two[at], ks + 1)
+        det = first * second - cross * cross
+        inverse = 1.0 / det
+        ratio = 1.0 / first
+        below = range(at, blocks)
+        u = {b: second * one[b] - cross * two[b] for b in below}
+        v = {b: first * two[b] - cross * one[b] for b in below}
+        us = {b: u[b] * inverse for b in below}
+        vs = {b: v[b] * inverse for b in below}
+        for i in range(k + 2, len(cols)):
+            left, right = spread(one[i // 8], i % 8), spread(two[i // 8], i % 8)
             for b in range(i // 8, blocks):
-                cols[i][b] = cols[i][b] - factor[b] * beside
-        factor[at] = jnp.where(sub > ks, factor[at], 0.0)
-        for t in range(2):
-            row = spread(parts[at][t], ks)
-            for b in range(at, blocks):
-                parts[b][t] = parts[b][t] - factor[b] * row
-    return jnp.concatenate(
-        [jnp.concatenate([parts[b][t] * scale[b] for t in range(2)], axis=1) for b in range(blocks)], axis=0
-    )
+                if i < k + 4:
+                    cols[i][b] = cols[i][b] - (u[b] * left + v[b] * right) * inverse
+                else:
+                    cols[i][b] = cols[i][b] - (us[b] * left + vs[b] * right)
+        scale[at] = jnp.where(sub == ks, lax.rsqrt(first), scale[at])
+        scale[at] = jnp.where(sub == ks + 1, lax.rsqrt(det * ratio), scale[at])
+        us[at] = jnp.where(sub > ks + 1, us[at], jnp.where(sub == ks + 1, cross * ratio, 0.0))
+        vs[at] = jnp.where(sub > ks + 1, vs[at], 0.0)
+        here, next_to = lane == start + k, lane == start + k + 1
+        left = jnp.where(here, 1.0, jnp.where(next_to, 0.0, spread(parts[at], ks)))
+        right = jnp.where(here, 0.0, jnp.where(next_to, 1.0, spread(parts[at], ks + 1)))
+        fresh = (here & (sub >= ks)) | (next_to & (sub >= ks + 1))
+        unit = (here & (sub == ks)) | (next_to & (sub == ks + 1))
+        parts[at] = jnp.where(fresh, unit.astype(f32), parts[at]) - (us[at] * left + vs[at] * right)
+        for b in range(at + 1, blocks):
+            parts[b] = jnp.where(here | next_to, 0.0, parts[b]) - (us[b] * left + vs[b] * right)
+    return jnp.concatenate([parts[b] * scale[b] for b in range(blocks)], axis=0)
 
 
 def factor_diag(work, rows):
+    row = lax.broadcasted_iota(jnp.int32, (STEP, 128), 0)
+    lane = lax.broadcasted_iota(jnp.int32, (STEP, 128), 1)
     for start in range(0, 128, STEP):
         after = start + STEP
         done = pivots(work, start)
         rows[start:after, :] = done
         if after < 128:
-            change = dot_tn(triple(done[:, :128], "hhl", 0), triple(done, "hlh", 0))
-            work[after:128, :] = work[after:128, :] - change[after:128, :]
+            right = jnp.where((lane < after) & (lane > start + row), 0.0, done)
+            change = dot_tn(triple(done, "hhl", 0), triple(right, "hlh", 0))
+            group = lax.broadcasted_iota(jnp.int32, (128 - after, 128), 1)
+            group = (group >= start) & (group < after)
+            work[after:128, :] = jnp.where(group, 0.0, work[after:128, :]) - change[after:128, :]
 
 
 def edge_rows(own, samples):
@@ -204,15 +223,23 @@
         gram[at] = gram[at] + dot_tn(edges[:, at[0]], edges[:, at[1]]) * (1.0 / TOTAL)
     above = lax.broadcasted_iota(jnp.int32, (128, 128), 1)
     below = lax.broadcasted_iota(jnp.int32, (128, 128), 0)
+    diagonals = [jnp.where(above == below, gram[128 * p : 128 * p + 128, 128 * p : 128 * p + 128], 0.0) for p in range(4)]
+    inward = [lax.rsqrt(jnp.sum(d, axis=0, keepdims=True)) for d in diagonals]
+    outward = [1.0 / v for v in inward]
+    for p in range(4):
+        rows_in = lax.rsqrt(jnp.sum(diagonals[p], axis=1, keepdims=True))
+        for q in range(p, 4):
+            at = slice(128 * p, 128 * p + 128), slice(128 * q, 128 * q + 128)
+            gram[at] = gram[at] * rows_in * inward[q]
     for p in range(4):
         lo, hi = 128 * p, 128 * p + 128
-        work[:, 0:128] = gram[lo:hi, lo:hi]
-        work[:, 128:256] = (above == below).astype(f32)
+        work[...] = gram[lo:hi, lo:hi]
         factor_diag(work, rows)
-        upper[lo:hi, lo:hi] = jnp.where(above >= below, rows[:, 0:128], 0.0)
+        both = rows[...]
+        upper[lo:hi, lo:hi] = jnp.where(above > below, both, jnp.where(above == below, 1.0 / both, 0.0)) * outward[p]
         if p > 0:
             upper[lo:hi, 0:lo] = jnp.zeros((128, lo), f32)
-        inverse = jnp.where(above <= below, rows[:, 128:256], 0.0)
+        inverse = jnp.where(above <= below, both, 0.0)
         stacked = triple(inverse, "hhl", 1)
         if p > 0:
             left = dot_nn(stacked, triple(behind[lo:hi, 0:lo], "hlh", 0))
@@ -221,7 +248,7 @@
             full = inverse
         if p < 3:
             right = dot_nn(stacked, triple(gram[lo:hi, hi:512], "hlh", 0))
-            upper[lo:hi, hi:512] = right
+            upper[lo:hi, hi:512] = right * jnp.concatenate(outward[p + 1 :], axis=1)
             first, second = triple(right, "hhl", 0), triple(right, "hlh", 0)
             for q in range(p + 1, 4):
                 a = 128 * (q - p - 1)
@@ -231,7 +258,7 @@
             if p > 0:
                 behind[hi:512, 0:lo] = behind[hi:512, 0:lo] - change[:, 0:lo]
             behind[hi:512, lo:hi] = -change[:, lo:hi]
-        high, low = split(full)
+        high, low = split(full * jnp.concatenate(inward[: p + 1], axis=1))
         basis[:, lo:hi] = (dot_nt(hankel[:, 0:hi], high) + dot_nt(hankel[:, 0:hi], low)).astype(bf16)
 
 
@@ -242,8 +269,8 @@
         in_specs=[SMEM, VMEM, VMEM, VMEM],
         scratch_shapes=[
             pltpu.VMEM((COLS, COLS), f32),
-            pltpu.VMEM((128, 256), f32),
-            pltpu.VMEM((128, 256), f32),
+            pltpu.VMEM((128, 128), f32),
+            pltpu.VMEM((128, 128), f32),
             pltpu.VMEM((COLS, 384), f32),
             pltpu.VMEM((4 * OWNERS, 128), f32),
             pltpu.VMEM((ROWS, COLS), bf16),

time: 107 us -> 105 us (0.981)
  Pallas kernels: 16.6 us -> 15.4 us
    pallas_call x1, Pallas kernels: 14.9 us -> 13.7 us  [factor(): pl.pallas_call(factor_kernel, out_shape=(jax.ShapeDtypeStruct((COLS, COLS...]
where the time goes in v4:
time: 105 us
  blocking collectives  78.4 us (75%)
  Pallas kernels  15.4 us (15%)
  starting transfers between devices  6.73 us (6%)
  local copies, waits for them, and re-layouts  1.79 us (2%)
  waiting for transfers between devices  1.33 us (1%)
  between operations  1.32 us (1%)
    all_to_all x1, blocking collectives, shards(): lax.all_to_all(sent, DEV, 0, 0, tiled=True).reshape(CHANNELS, WINDOW)  33.7 us
    all_to_all x1, blocking collectives, shards(): parts = lax.all_to_all(parts, 'zh', 0, 0, tiled=True)  16.6 us
    all_to_all x1, blocking collectives, shards(): parts = lax.all_to_all(packed, OWNER, 0, 0, tiled=True)  16 us
    pallas_call x1, Pallas kernels, factor(): pl.pallas_call(factor_kernel, out_shape=(jax.ShapeDtypeStruct((COLS, COLS...  13.7 us
    all_to_all x1, blocking collectives, shards(): own = lax.all_to_all(parts, OWNER, 0, 0, tiled=True)  12.1 us
    ppermute x1, starting transfers between devices, shards(): other = lax.ppermute(own, 'core', [(0, 1), (1, 0)])  6.73 us
  transfers between devices with their start and end apart: 1, of which 1 were waited for; matrix products, arithmetic and copies ran while one was open for 0% of the time, Pallas kernels for 0%

profile of v4, /device:TPU:1, one launch (start us, length us, event | category | flops | bytes accessed | tf_op | source)
XLA Modules:
  0.0 105.0 jit_solution(7124529826689041984)
XLA Ops:
  1.3 0.1 pad_add_fusion.place
  1.4 0.0 copy-start
  1.4 0.9 copy-done
  2.3 0.0 copy-start.1
  2.3 0.8 copy-done.1
  3.1 0.6 pack.1
  3.7 33.7 %all_to_all.20 = bf16[32,4,640]{2,1,0:T(4,128)(2,1)S(1)} all-to-all(bf16[32,4,640]{2,1,0:T(4,128)(2,1)S(1)} %pack.1), channel_id=1, replica_groups=mesh['x'=4,'y'=4,'zh'=8,'zl'=2,'core'=2] {'zh','zl','core'}, dimensions={0} | all-to-all | bytes 327680 | tf_op jit(solution)/shard_map/all_to_all | solution.py:296
  37.4 1.1 %partial_gram.1 = (f32[32,20,128]{2,1,0:T(8,128)S(1)}, bf16[256,512]{1,0:T(8,128)(2,1)S(1)}, f32[8,128]{1,0:T(8,128)S(1)}) custom-call(s32[3]{0:T(128)S(1)} %pad_add_fusion.place, bf16[128,640]{1,0:T(8,128)(2,1)S(1)} %reshape.7.series), custom_call_target="tpu_custom_call" | custom-call | tf_op jit(solution)/shard_map/partial_gram/pallas_call | solution.py:297
  38.5 16.0 %all_to_all.21.parts = f32[32,20,128]{2,1,0:T(8,128)S(1)} all-to-all(f32[32,20,128]{2,1,0:T(8,128)S(1)} %get-tuple-element.5), channel_id=1, replica_groups=mesh['x'=4,'y'=4,'zh'=8,'zl'=2,'core'=2] {'x','y','zl'}, dimensions={0} | all-to-all | bytes 655360 | tf_op jit(solution)/shard_map/all_to_all | solution.py:308
  54.5 16.6 %all_to_all.22.parts = f32[8,24,128]{2,1,0:T(8,128)S(1)} all-to-all(f32[8,24,128]{2,1,0:T(8,128)S(1)} %add_owners.1), channel_id=1, replica_groups=mesh['x'=4,'y'=4,'zh'=8,'zl'=2,'core'=2] {'zh'}, dimensions={0} | all-to-all | bytes 196608 | tf_op jit(solution)/shard_map/all_to_all | solution.py:310
  71.2 12.1 %all_to_all.23.own = f32[32,24,128]{2,1,0:T(8,128)S(1)} all-to-all(f32[32,24,128]{2,1,0:T(8,128)S(1)} %add_planes.1), channel_id=1, replica_groups=mesh['x'=4,'y'=4,'zh'=8,'zl'=2,'core'=2] {'x','y','zl'}, dimensions={0} | all-to-all | bytes 786432 | tf_op jit(solution)/shard_map/all_to_all | solution.py:312
  83.2 6.7 %collective-permute-start = (f32[32,24,128]{2,1,0:T(8,128)S(1)}, f32[32,24,128]{2,1,0:T(8,128)S(1)}, u32[]{:S(2)}, u32[]{:S(2)}) collective-permute-start(f32[32,24,128]{2,1,0:T(8,128)S(1)} %all_to_all.23.own), channel_id=1, source_target_pairs={{0,1},{1,0},{2,3},{3,2},{4,5},{5,4},{6,7},{7,6},{8,9},{9,8},{10,11... | collective-permute-start | bytes 1179656 | tf_op jit(solution)/shard_map/ppermute | solution.py:313
  90.0 1.3 %collective-permute-done.other = f32[32,24,128]{2,1,0:T(8,128)S(1)} collective-permute-done((f32[32,24,128]{2,1,0:T(8,128)S(1)}, f32[32,24,128]{2,1,0:T(8,128)S(1)}, u32[]{:S(2)}, u32[]{:S(2)}) %collective-permute-start) | collective-permute-done | bytes 393248 | tf_op jit(solution)/shard_map/ppermute | solution.py:313
  91.3 13.7 %factor.1 = (f32[512,512]{1,0:T(8,128)}, bf16[256,512]{1,0:T(8,128)(2,1)}) custom-call(s32[3]{0:T(128)S(1)} %pad_add_fusion.place, f32[32,24,128]{2,1,0:T(8,128)S(1)} %all_to_all.23.own, f32[32,24,128]{2,1,0:T(8,128)S(1)} %collective-permute-done.other, bf16[256,512]{1,0:T(8,128)(2,1)S(1)} %get-tuple-element.7.hankel_in), custom_call_target="tpu_custom_call" | custom-call | tf_op jit(solution)/shard_map/factor/pallas_call | solution.py:266
  (3 shorter events, 0.1 us)
Async XLA Ops:
  1.4 0.9 copy-start
  2.3 0.8 copy-start.1
  83.2 8.1 %collective-permute-start = (f32[32,24,128]{2,1,0:T(8,128)S(1)}, f32[32,24,128]{2,1,0:T(8,128)S(1)}, u32[]{:S(2)}, u32[]{:S(2)}) collective-permute-start(f32[32,24,128]{2,1,0:T(8,128)S(1)} %all_to_all.23.own), channel_id=1, source_target_pairs={{0,1},{1,0},{2,3},{3,2},{4,5},{5,4},{6,7},{7,6},{8,9},{9,8},{10,11... | collective-permute-start | bytes 1179656 | tf_op jit(solution)/shard_map/ppermute | solution.py:313
